TPU v7x, 256 devices: a whole 4x4x8 slice. The times are simulated.
256 devices in a mesh: req: 4 (over x_lo, core), ctx: 64 (over x_hi, z, y).
Axes of the slice: x: 4 (x_hi: 2, x_lo: 2; x = x_hi * 2 + x_lo), y: 4, z: 8, core: 2. Of those that a mesh axis runs over, the one named last changes fastest.
Arguments:
- queries: bfloat16 [4, 64, 64, 6144], P('req', 'ctx'), may hold values from -160 to 160, as said below
- keys: bfloat16 [4, 32768, 128], P('req', 'ctx'), may hold values from -6 to 6
- values: bfloat16 [4, 32768, 128], P('req', 'ctx'), may hold values from -6 to 6
- query_host: int32 [4], P('req'), may hold values from 0 to 63
- lengths: int32 [4, 64], P('req', 'ctx'), may hold values from 1 to 4, as said below
Outputs:
- attended: bfloat16 [4, 64, 6144], P('req')
- log_total: float32 [4, 64, 48], P('req', 'ctx')
Inputs may be any that keep to these rules, and one draw needn't show every extreme that they name: Each request's queries; every entry within the range. `lengths`: number of leading valid 128-token blocks in a device's slots; every device has at least one, and in every request some device is full (4) and some device has exactly one.
All inputs are finite; a program needn't handle non-finite values.
Results may differ from a plain program's by a relative error of at most 0.0044.
Values may be sent and summed in bfloat16 or wider, within the bound.
A program may use at most 256 MiB of HBM per device.

v0:
```python
import jax
import jax.numpy as jnp
from jax import lax
from jax.sharding import PartitionSpec as P

H = 48
DH = 128


NEG = -1e30


def broadcast(value, axis, source):
    kept = jnp.where(lax.axis_index(axis) == source, value, 0).astype(value.dtype)
    return lax.psum(kept, axis)


def body(queries, keys, values, query_host, lengths):
    q_tok = queries.shape[2]
    ctx_dev = keys.shape[1]
    steps_dev = ctx_dev // 256
    local = broadcast(queries[0, 0], "ctx", query_host[0])
    query_matrix = local.reshape(q_tok, H, DH)
    key_steps = keys[0].reshape(steps_dev, 2, 128, DH)
    value_steps = values[0].reshape(steps_dev, 2, 128, DH)
    block_ids = jnp.arange(steps_dev * 2, dtype=jnp.int32).reshape(steps_dev, 2)
    valid = (block_ids < lengths[0, 0]).astype(jnp.float32)
    softmax_scale = float(DH) ** (-0.5)

    def step(carry, item):
        top, total, numer = carry
        key_block_slice, value_block_slice, ok = item
        logit_scores = (
            jnp.einsum(
                "jgv,tfv->jgtf", query_matrix, key_block_slice, preferred_element_type=jnp.float32
            )
            * softmax_scale
        )
        block_max = jnp.max(logit_scores, axis=-1)
        expo = jnp.exp(logit_scores - block_max[..., None])
        block_total = jnp.sum(expo, axis=-1)
        attention_weights = expo.astype(jnp.bfloat16)
        block_result = jnp.einsum(
            "zcgn,gna->zcga",
            attention_weights,
            value_block_slice,
            preferred_element_type=jnp.float32,
        )
        block_max = jnp.where(ok[None, None, :] > 0, block_max, NEG)
        new_top = jnp.maximum(top, jnp.max(block_max, axis=-1))
        keep = jnp.exp(top - new_top)
        factor = jnp.exp(block_max - new_top[..., None]) * ok[None, None, :]
        total = total * keep + jnp.sum(block_total * factor, axis=-1)
        numer = numer * keep[..., None] + jnp.sum(block_result * factor[..., None], axis=2)
        return ((new_top, total, numer), None)

    start = (
        jnp.full((q_tok, H), NEG, jnp.float32),
        jnp.zeros((q_tok, H), jnp.float32),
        jnp.zeros((q_tok, H, DH), jnp.float32),
    )
    (top, total, numer), _ = lax.scan(step, start, (key_steps, value_steps, valid))
    share = q_tok // lax.axis_size("ctx")
    offset = lax.axis_index("ctx") * share
    overall = lax.pmax(top, "ctx")
    factor = jnp.exp(top - overall)
    numer_rows, total_rows = (
        lax.psum_scatter(numer * factor[..., None], "ctx", scatter_dimension=0, tiled=True),
        lax.psum_scatter(total * factor, "ctx", scatter_dimension=0, tiled=True),
    )
    finished = (numer_rows / total_rows[..., None]).astype(jnp.bfloat16).reshape(share, H * DH)
    log_total = lax.dynamic_slice_in_dim(overall, offset, share, 0) + jnp.log(total_rows)
    attended = lax.all_gather(finished, "ctx", axis=0, tiled=True)
    return (attended[None], log_total[None])


def solution(mesh):
    return jax.shard_map(
        body,
        mesh=mesh,
        in_specs=(
            P("req", "ctx", None, None),
            P("req", "ctx", None),
            P("req", "ctx", None),
            P("req"),
            P("req", "ctx"),
        ),
        out_specs=(P("req", None, None), P("req", "ctx", None)),
        check_vma=False,
    )
```

profile of v0, /device:TPU:2, one launch (start us, length us, event | category | flops | bytes accessed | tf_op | source)
XLA Modules:
  0.0 2047.3 jit_solution(6969553502498895969)
XLA Ops:
  7.2 0.0 all-reduce.3.cloned.1.call-start
  7.9 0.1 select_bitcast_fusion
  7.9 1.0 copy.22
  9.0 0.0 reduce-scatter.3.cloned.1.call-start
  9.7 670.8 %all-reduce.3.cloned.1.call-done = bf16[64,48,128]{2,1,0:T(8,128)(2,1)} async-done(((bf16[64,48,128]{2,1,0:T(8,128)(2,1)}), bf16[64,48,128]{2,1,0:T(8,128)(2,1)}) %all-reduce.3.cloned.1.call-update) | async-done | bytes 786448 | tf_op jit(solution)/shard_map/psum | solution.py:15
  680.5 2.2 copy.14
  682.7 18.6 while.15
  682.7 2.2 bitcast_reduce_fusion.2
  684.9 1.8 fusion.29
  686.8 0.1 select_reduce_fusion.2
  686.8 0.1 multiply_reduce_fusion.2
  687.0 3.1 fusion.31
  690.1 0.8 fusion.32
  690.9 1.1 copy-done.1
  692.0 2.2 bitcast_reduce_fusion.2
  694.2 1.8 fusion.29
  696.1 0.1 select_reduce_fusion.2
  696.2 0.1 multiply_reduce_fusion.2
  696.3 3.1 fusion.31
  699.4 0.8 fusion.32
  700.2 1.1 copy-done.1
  701.3 354.1 %pmax.7 = f32[64,48]{0,1:T(8,128)S(1)} all-reduce(f32[64,48]{0,1:T(8,128)S(1)} %get-tuple-element.47), channel_id=1, replica_groups=mesh['req'=4,'ctx'=64] {'ctx'}, use_global_device_ids=true, to_apply=%region_8.9 | all-reduce | flops 3072 | bytes 24576 | tf_op jit(solution)/shard_map/pmax | solution.py:65
  1055.5 0.1 copy.15
  1055.5 3.6 copy_multiply_fusion
  1059.2 0.6 copy-done.3
  1059.8 0.6 dynamic-slice
  1060.4 350.9 %all-reduce = f32[64,48]{0,1:T(8,128)S(1)} all-reduce(f32[64,48]{0,1:T(8,128)S(1)} %get-tuple-element.132), channel_id=3, replica_groups=mesh['req'=4,'ctx'=64] {'ctx'}, use_global_device_ids=true, to_apply=%region_10.11.clone | all-reduce | flops 3072 | bytes 24576
  1411.3 1.3 add_reduce_fusion
  1412.7 438.6 %reduce-scatter.3.cloned.1.call-done = f32[1,48,128]{2,1,0:T(8,128)} async-done(((f32[64,48,128]{2,1,0:T(8,128)}), f32[1,48,128]{2,1,0:T(8,128)}) %reduce-scatter.3.cloned.1.call-update) | async-done | bytes 24592 | tf_op jit(solution)/shard_map/reduce_scatter | solution.py:68
  1851.2 0.8 divide_convert_fusion
  1852.1 187.1 %all-gather = bf16[64,1,6144]{2,1,0:T(2,128)(2,1)S(1)} all-gather(bf16[1,1,6144]{2,1,0:T(2,128)(2,1)S(1)} %reshape.48), channel_id=1, replica_groups=mesh['req'=4,'ctx'=64] {'ctx'}, dimensions={0}, use_global_device_ids=true | all-gather | bytes 798720 | tf_op jit(solution)/shard_map/all_gather | solution.py:73
  2039.1 1.3 copy.25
  (25 shorter events, 0.2 us)
Async XLA Ops:
  7.2 673.3 %all-reduce.3.cloned.1.call-start = ((), (), s32[]{:S(2)}) async-start(), calls=%async_computation.1 | async-start | bytes 1572864 | tf_op jit(solution)/shard_map/psum | solution.py:15
  8.9 673.8 %copy-start.2 = (bf16[1,512,128]{2,1,0:T(8,128)(2,1)S(1)}, bf16[1,512,128]{2,1,0:T(8,128)(2,1)}, u32[]{:S(2)}) copy-start(bf16[1,512,128]{2,1,0:T(8,128)(2,1)} %param.8) | copy-start | bytes 393220
  9.0 1842.2 %reduce-scatter.3.cloned.1.call-start = ((), (), s32[]{:S(2)}) async-start(), calls=%async_computation.2 | async-start | bytes 1597440 | tf_op jit(solution)/shard_map/reduce_scatter | solution.py:68
  687.0 3.1 copy-start
  690.9 1.2 copy-start.1
  696.3 3.1 copy-start
  700.2 1.2 copy-start.1
  1059.1 0.7 copy-start.3
Sparse Core Ops, SparseCore 0:
  11.2 669.2 all-reduce.2
  1059.3 791.8 reduce-scatter.2
where the time goes:
time: 2050 us
  waiting for transfers between devices  1110 us (54%)
  blocking collectives  892 us (44%)
    psum x1, waiting for transfers between devices, broadcast(): return lax.psum(kept, axis)  671 us
    reduce_scatter x1, waiting for transfers between devices, body(): lax.psum_scatter(numer * factor[..., None], 'ctx', scatter_dimension=0, t...  439 us
    pmax x1, blocking collectives, body(): overall = lax.pmax(top, 'ctx')  354 us
    unnamed x1, blocking collectives  351 us
    all_gather x1, blocking collectives, body(): attended = lax.all_gather(finished, 'ctx', axis=0, tiled=True)  187 us
  transfers between devices with their start and end apart: 2, of which 2 were waited for; matrix products, arithmetic and copies ran while one was open for 0% of the time, Pallas kernels for 0%

commit v1 on v0

v1 whole, which is shorter than its diff:
```python
import math

import jax
import jax.numpy as jnp
from jax import lax
from jax.experimental import pallas as pl
from jax.experimental.pallas import tpu as pltpu
from jax.sharding import PartitionSpec as P


H = 48
DH = 128
T = 64
KEYS = 512
BLOCK = 128
HD = H * DH
NZ = 8
NXY = 8
ROWS = 384
PIECE = 48
A_COLS = 4096
NEG = -1e30
LOG2E = math.log2(math.e)
LN2 = math.log(2.0)
SCALE = DH ** -0.5 * LOG2E
MESH = pl.DeviceIdType.MESH


def kernel(host_ref, len_ref, q_ref, k_ref, v_ref, out_ref, log_ref,
           kv, s1a, s1b, x2a, x2b, s2a, s2b, qg, qm, acc, top, po, ps, o_in, st_in, lg,
           loc_sem, kv_send, kv_recv, send, recv):
    me = lax.axis_index("ctx")
    x, z, y = me // 32, (me // 4) % 8, me % 4
    xy = x * 4 + y
    tg, hg = z // 2, z % 2

    def z_of(k):
        return lax.rem(z + k, NZ)

    def at_z(zz):
        return {"ctx": x * 32 + zz * 4 + y}

    def xy_to(k):
        px, py = lax.rem(x + k // 4, 2), lax.rem(y + k % 4, 4)
        return px * 4 + py, {"ctx": px * 32 + z * 4 + py}

    def put(src, dst, stage, device):
        pltpu.make_async_remote_copy(
            src_ref=src, dst_ref=dst, send_sem=send.at[stage], recv_sem=recv.at[stage],
            device_id=device, device_id_type=MESH).start()

    def both(stage, like):
        return pltpu.make_async_remote_copy(
            src_ref=like, dst_ref=like, send_sem=send.at[stage], recv_sem=recv.at[stage],
            device_id=at_z(z_of(1)), device_id_type=MESH)

    def cols(start, n):
        return pl.ds(pl.multiple_of(start, 128), n)

    def rows(start, n):
        return pl.ds(pl.multiple_of(start, 16), n)

    z_order = (4, 3, 5, 2, 6, 1, 7)
    xy_order = (6, 5, 7, 2, 4, 1, 3)

    def a_chunk(c):
        return q_ref.at[:, cols(c * 512, 512)]

    def b_chunk(zz):
        return q_ref.at[rows((zz // 2) * 16, 16), cols(A_COLS + lax.rem(zz, 2) * 1024, 1024)]

    local = [
        pltpu.make_async_copy(k_ref, kv.at[xy, pl.ds(0, KEYS)], loc_sem.at[0]),
        pltpu.make_async_copy(v_ref, kv.at[xy, pl.ds(KEYS, KEYS)], loc_sem.at[1]),
        pltpu.make_async_copy(a_chunk(xy), s1a.at[xy], loc_sem.at[2]),
        pltpu.make_async_copy(b_chunk(z), s1b.at[z], loc_sem.at[3]),
    ]
    for copy in local:
        copy.start()

    barrier = pltpu.get_barrier_semaphore()
    for k in range(1, NZ):
        pl.semaphore_signal(barrier, inc=1, device_id=at_z(z_of(k)), device_id_type=MESH)
    for k in range(1, NXY):
        pl.semaphore_signal(barrier, inc=1, device_id=xy_to(k)[1], device_id_type=MESH)
    length = len_ref[0, 0].astype(jnp.float32)
    kv[xy, 2 * KEYS:, :] = jnp.full((16, DH), length, jnp.float32).astype(jnp.bfloat16)
    pl.semaphore_wait(barrier, 14)

    for k in xy_order:
        c, device = xy_to(k)
        put(a_chunk(c), s1a.at[xy], 0, device)
    for k in z_order:
        zz = z_of(k)
        put(b_chunk(zz), s1b.at[z], 1, at_z(zz))
    local[0].wait()
    local[1].wait()

    def kv_copy(k):
        return pltpu.make_async_remote_copy(
            src_ref=kv.at[xy], dst_ref=kv.at[xy], send_sem=kv_send.at[k], recv_sem=kv_recv.at[k],
            device_id=xy_to(k)[1], device_id_type=MESH)

    for k in range(1, NXY):
        kv_copy(k).start()

    host = host_ref[0]
    host_z = lax.rem(host // 4, 8)
    host_xy = host // 32 * 4 + lax.rem(host, 4)

    local[2].wait()
    both(0, s1a.at[pl.ds(0, 7)]).wait_recv()
    chunk = s1a[host_xy]
    for p in range(NZ):
        a, b = p // 2, p % 2
        x2a[p] = chunk[16 * a:16 * a + 16, 256 * b:256 * b + 256]
    s2a[z] = x2a[z]
    for k in z_order:
        zz = z_of(k)
        put(x2a.at[zz], s2a.at[z], 2, at_z(zz))
    local[3].wait()
    both(1, s1b.at[pl.ds(0, 7)]).wait_recv()
    chunk = s1b[host_z]
    for p in range(NXY):
        x2b[p] = chunk[:, 128 * p:128 * p + 128]
    s2b[xy] = x2b[xy]
    for k in xy_order:
        c, device = xy_to(k)
        put(x2b.at[c], s2b.at[xy], 3, device)

    both(2, s2a.at[pl.ds(0, 7)]).wait_recv()
    both(3, s2b.at[pl.ds(0, 7)]).wait_recv()
    qg[z, :, 0:256] = s2a[host_z]
    qg[z, :, 256:384] = s2b[host_xy]
    for k in z_order:
        put(qg.at[z], qg.at[z], 4, at_z(z_of(k)))
    both(4, qg.at[pl.ds(0, 7)]).wait_recv()
    for p in range(NZ):
        for c in range(3):
            qm[PIECE * p + 16 * c:PIECE * p + 16 * c + 16, :] = qg[p, :, 128 * c:128 * c + 128]

    acc[...] = jnp.zeros_like(acc)
    top[...] = jnp.full(top.shape, NEG, jnp.float32)
    block_id = lax.broadcasted_iota(jnp.int32, (1, KEYS), 1) // BLOCK

    def attend(c):
        valid = kv[c, 2 * KEYS:2 * KEYS + 16, :].astype(jnp.float32)[0:1, :]
        valid = jnp.concatenate([valid] * (KEYS // DH), axis=1)
        score = lax.dot_general(
            qm[...], kv[c, 0:KEYS, :], (((1,), (1,)), ((), ())), preferred_element_type=jnp.float32)
        score = jnp.where(block_id.astype(jnp.float32) < valid, score * SCALE, NEG)
        old = top[:, 0:1]
        new = jnp.maximum(old, jnp.max(score, axis=1, keepdims=True))
        weight = jnp.exp2(score - new).astype(jnp.bfloat16)
        value = jnp.concatenate(
            [kv[c, KEYS:2 * KEYS, :], jnp.ones((KEYS, DH), jnp.bfloat16)], axis=1)
        acc[...] = acc[...] * jnp.exp2(old - new) + jnp.dot(
            weight, value, preferred_element_type=jnp.float32)
        top[...] = jnp.broadcast_to(new, top.shape)

    attend(xy)

    def step(k, carry):
        c = lax.rem(x + k // 4, 2) * 4 + lax.rem(y - lax.rem(k, 4) + 4, 4)
        pltpu.make_async_remote_copy(
            src_ref=kv.at[c], dst_ref=kv.at[c], send_sem=kv_send.at[k], recv_sem=kv_recv.at[k],
            device_id=at_z(z_of(1)), device_id_type=MESH).wait_recv()
        attend(c)
        return carry

    lax.fori_loop(1, NXY, step, 0)

    total = acc[:, DH:]
    po[...] = (acc[:, :DH] / total).astype(jnp.bfloat16).reshape(NZ, PIECE, DH)
    lse = top[...] + jnp.log(total) * LOG2E
    lane = lax.broadcasted_iota(jnp.int32, (PIECE, DH), 1)
    diagonal = lane == lax.broadcasted_iota(jnp.int32, (PIECE, DH), 0)
    for p in range(NZ):
        part = lse[PIECE * p:PIECE * p + PIECE, :]
        ps[p] = jnp.sum(jnp.where(diagonal, part, 0.0), axis=0, keepdims=True)
    o_in[z] = po[z]
    st_in[z] = ps[z]
    for k in z_order:
        zz = z_of(k)
        put(po.at[zz], o_in.at[z], 5, at_z(zz))
        put(ps.at[zz], st_in.at[z], 6, at_z(zz))
    both(6, st_in.at[pl.ds(0, 7)]).wait_recv()
    stat = jnp.concatenate([st_in[s] for s in range(NZ)], axis=0)
    overall = jnp.max(stat, axis=0, keepdims=True)
    share = jnp.exp2(stat - overall)
    summed = jnp.sum(share, axis=0, keepdims=True)
    share = share / summed
    lg[xy, z] = overall * LN2 + jnp.log(summed)
    both(5, o_in.at[pl.ds(0, 7)]).wait_recv()
    result = jnp.zeros((PIECE, DH), jnp.float32)
    for s in range(NZ):
        column = jnp.sum(jnp.where(diagonal, share[s:s + 1, :], 0.0), axis=1, keepdims=True)
        result = result + column * o_in[s].astype(jnp.float32)
    result = result.astype(jnp.bfloat16)

    mine = rows(tg * 16, 16)
    a_here = out_ref.at[mine, cols(xy * 512 + hg * 256, 256)]
    b_here = out_ref.at[mine, cols(A_COLS + hg * 1024 + xy * 128, 128)]
    out_ref[mine, cols(xy * 512 + hg * 256, 128)] = result[0:16]
    out_ref[mine, cols(xy * 512 + hg * 256 + 128, 128)] = result[16:32]
    out_ref[mine, cols(A_COLS + hg * 1024 + xy * 128, 128)] = result[32:48]
    for k in z_order:
        put(a_here, a_here, 7, at_z(z_of(k)))
    for k in xy_order:
        put(b_here, b_here, 8, xy_to(k)[1])
    for k in z_order:
        put(lg.at[xy, z], lg.at[xy, z], 9, at_z(z_of(k)))
    both(7, s2a.at[pl.ds(0, 7)]).wait_recv()
    a_all = out_ref.at[:, cols(xy * 512, 512)]
    for k in xy_order:
        put(a_all, a_all, 10, xy_to(k)[1])
    both(8, s2b.at[pl.ds(0, 7)]).wait_recv()
    b_all = out_ref.at[mine, cols(A_COLS + hg * 1024, 1024)]
    for k in z_order:
        put(b_all, b_all, 11, at_z(z_of(k)))
    both(9, st_in.at[pl.ds(0, 7)]).wait_recv()
    for k in xy_order:
        put(lg.at[xy], lg.at[xy], 12, xy_to(k)[1])

    both(12, lg.at[pl.ds(0, 7)]).wait_recv()
    t_group, t_in = me // 16, lax.rem(me, 16)
    lane = lax.broadcasted_iota(jnp.int32, (NXY, DH), 1)
    source = lax.broadcasted_iota(jnp.int32, (NXY, DH), 0)
    logs = jnp.zeros((NXY, DH), jnp.float32)
    for b in range(2):
        part = jnp.concatenate([lg[c, 2 * t_group + b] for c in range(NXY)], axis=0)
        for c in range(3):
            column = jnp.sum(jnp.where(lane == 16 * c + t_in, part, 0.0), axis=1, keepdims=True)
            head = source * 4 + 2 * b + c if c < 2 else 32 + 8 * b + source
            logs = logs + jnp.where(lane == head, column, 0.0)
    log_ref[...] = jnp.sum(logs, axis=0, keepdims=True)[:, :H]

    both(10, s1a.at[pl.ds(0, 7)]).wait_recv()
    both(11, s1b.at[pl.ds(0, 7)]).wait_recv()
    for stage, like in enumerate((s1a, s1b, s2a, s2b, qg, o_in, st_in, s2a, s2b, st_in, s1a, s1b, lg)):
        both(stage, like.at[pl.ds(0, 7)]).wait_send()
    for k in range(1, NXY):
        kv_copy(k).wait_send()


def body(queries, keys, values, query_host, lengths):
    bf16, f32 = jnp.bfloat16, jnp.float32
    attended, log_total = pl.pallas_call(
        kernel,
        out_shape=(
            jax.ShapeDtypeStruct((T, HD), bf16),
            jax.ShapeDtypeStruct((1, H), f32),
        ),
        in_specs=[
            pl.BlockSpec(memory_space=pltpu.SMEM),
            pl.BlockSpec(memory_space=pltpu.SMEM),
            pl.BlockSpec(memory_space=pl.ANY),
            pl.BlockSpec(memory_space=pl.ANY),
            pl.BlockSpec(memory_space=pl.ANY),
        ],
        out_specs=(
            pl.BlockSpec(memory_space=pltpu.VMEM),
            pl.BlockSpec(memory_space=pltpu.VMEM),
        ),
        scratch_shapes=[
            pltpu.VMEM((NXY, 2 * KEYS + 16, DH), bf16),
            pltpu.VMEM((NXY, T, 512), bf16),
            pltpu.VMEM((NZ, 16, 1024), bf16),
            pltpu.VMEM((NZ, 16, 256), bf16),
            pltpu.VMEM((NXY, 16, 128), bf16),
            pltpu.VMEM((NZ, 16, 256), bf16),
            pltpu.VMEM((NXY, 16, 128), bf16),
            pltpu.VMEM((NZ, 16, 384), bf16),
            pltpu.VMEM((ROWS, DH), bf16),
            pltpu.VMEM((ROWS, 2 * DH), f32),
            pltpu.VMEM((ROWS, DH), f32),
            pltpu.VMEM((NZ, PIECE, DH), bf16),
            pltpu.VMEM((NZ, 1, DH), f32),
            pltpu.VMEM((NZ, PIECE, DH), bf16),
            pltpu.VMEM((NZ, 1, DH), f32),
            pltpu.VMEM((NXY, NZ, 1, DH), f32),
            pltpu.SemaphoreType.DMA((4,)),
            pltpu.SemaphoreType.DMA((NXY,)),
            pltpu.SemaphoreType.DMA((NXY,)),
            pltpu.SemaphoreType.DMA((13,)),
            pltpu.SemaphoreType.DMA((13,)),
        ],
        compiler_params=pltpu.CompilerParams(
            collective_id=0, has_side_effects=True, vmem_limit_bytes=40 * 2**20),
    )(query_host, lengths, queries.reshape(T, HD), keys.reshape(KEYS, DH), values.reshape(KEYS, DH))
    return attended[None], log_total[None]


def solution(mesh):
    return jax.shard_map(
        body,
        mesh=mesh,
        in_specs=(
            P("req", "ctx", None, None),
            P("req", "ctx", None),
            P("req", "ctx", None),
            P("req"),
            P("req", "ctx"),
        ),
        out_specs=(P("req", None, None), P("req", "ctx", None)),
        check_vma=False,
    )
```

time: 2050 us -> 79.3 us (0.04)
  waiting for transfers between devices: 1110 us -> 0 us
  blocking collectives: 892 us -> 0 us
  Pallas kernels: 0 us -> 72.3 us
    psum x1 -> x0, waiting for transfers between devices: 671 us -> none  [broadcast(): return lax.psum(kept, axis)]
    reduce_scatter x1 -> x0, waiting for transfers between devices: 439 us -> none  [body(): lax.psum_scatter(numer * factor[..., None], 'ctx', scatter_dimension=0, t...]
    pmax x1 -> x0, blocking collectives: 354 us -> none  [body(): overall = lax.pmax(top, 'ctx')]
    unnamed x1 -> x0, blocking collectives: 351 us -> none
    all_gather x1 -> x0, blocking collectives: 187 us -> none  [body(): attended = lax.all_gather(finished, 'ctx', axis=0, tiled=True)]
    pallas_call x0 -> x1, Pallas kernels: none -> 72.3 us  [body(): pl.pallas_call(kernel, out_shape=(jax.ShapeDtypeStruct((T, HD), bf16), ja...]
  transfers between devices with their start and end apart: 2 -> 0, of which waited for: 2 -> 0; matrix products, arithmetic and copies ran while one was open for 0% -> 0% of each run, Pallas kernels for 0% -> 0%
where the time goes in v1:
time: 79.3 us; the launch traced here: 78.6 us
  Pallas kernels  72.3 us (91%)
  local copies, waits for them, and re-layouts  4.33 us (5%)
  between operations  1.94 us (2%)
    pallas_call x1, Pallas kernels, body(): pl.pallas_call(kernel, out_shape=(jax.ShapeDtypeStruct((T, HD), bf16), ja...  72.3 us
    unnamed x8, local copies, waits for them, and re-layouts  4.33 us

profile of v1, /device:TPU:2, one launch (start us, length us, event | category | flops | bytes accessed | tf_op | source)
XLA Modules:
  0.0 78.6 jit_solution(4710481314753424332)
XLA Ops:
  1.9 0.0 copy-start
  1.9 1.1 %copy-done = bf16[1,1,64,6144]{3,2,1,0:T(8,128)(2,1)S(1)} copy-done((bf16[1,1,64,6144]{3,2,1,0:T(8,128)(2,1)S(1)}, bf16[1,1,64,6144]{3,2,1,0:T(8,128)(2,1)}, u32[]{:S(2)}) %copy-start) | copy-done | bytes 786456
  3.1 0.0 copy-start.1
  3.1 0.9 %copy-done.1 = bf16[1,512,128]{2,1,0:T(8,128)(2,1)S(1)} copy-done((bf16[1,512,128]{2,1,0:T(8,128)(2,1)S(1)}, bf16[1,512,128]{2,1,0:T(8,128)(2,1)}, u32[]{:S(2)}) %copy-start.1) | copy-done | bytes 131096
  4.0 0.0 copy-start.2
  4.0 0.9 %copy-done.2 = bf16[1,512,128]{2,1,0:T(8,128)(2,1)S(1)} copy-done((bf16[1,512,128]{2,1,0:T(8,128)(2,1)S(1)}, bf16[1,512,128]{2,1,0:T(8,128)(2,1)}, u32[]{:S(2)}) %copy-start.2) | copy-done | bytes 131096
  4.9 72.3 %shard_map.68 = (bf16[64,6144]{1,0:T(8,128)(2,1)S(1)}, f32[1,48]{1,0:T(1,128)S(1)}) custom-call(s32[1]{0:T(128)S(6)} %copy.9.host_ref, s32[1,1]{1,0:T(1,128)S(6)} %copy.10.len_ref, bf16[64,6144]{1,0:T(8,128)(2,1)S(1)} %bitcast.5, bf16[512,128]{1,0:T(8,128)(2,1)S(1)} %bitcast.7, bf16[512,128]{1,0:T(8,128)(2,1)S(1)} %bitcast.8), custom_call_target="tpu_custom_call" | custom-call | tf_op jit(solution)/shard_map/pallas_call | solution.py:248
  77.2 0.9 %copy.11 = bf16[1,64,6144]{2,1,0:T(8,128)(2,1)} copy(bf16[1,64,6144]{2,1,0:T(8,128)(2,1)S(1)} %bitcast.6) | data formatting | bytes 1572864
  78.1 0.5 copy.12
Async XLA Ops:
  1.9 1.1 %copy-start = (bf16[1,1,64,6144]{3,2,1,0:T(8,128)(2,1)S(1)}, bf16[1,1,64,6144]{3,2,1,0:T(8,128)(2,1)}, u32[]{:S(2)}) copy-start(bf16[1,1,64,6144]{3,2,1,0:T(8,128)(2,1)} %param.5) | copy-start | bytes 2359300
  3.1 0.9 %copy-start.1 = (bf16[1,512,128]{2,1,0:T(8,128)(2,1)S(1)}, bf16[1,512,128]{2,1,0:T(8,128)(2,1)}, u32[]{:S(2)}) copy-start(bf16[1,512,128]{2,1,0:T(8,128)(2,1)} %param.6) | copy-start | bytes 393220
  4.0 0.9 %copy-start.2 = (bf16[1,512,128]{2,1,0:T(8,128)(2,1)S(1)}, bf16[1,512,128]{2,1,0:T(8,128)(2,1)}, u32[]{:S(2)}) copy-start(bf16[1,512,128]{2,1,0:T(8,128)(2,1)} %param.7) | copy-start | bytes 393220

commit v2 on v1

--- a/solution.py
+++ b/solution.py
@@ -26,9 +26,9 @@
 MESH = pl.DeviceIdType.MESH
 
 
-def kernel(host_ref, len_ref, q_ref, k_ref, v_ref, out_ref, log_ref,
-           kv, s1a, s1b, x2a, x2b, s2a, s2b, qg, qm, acc, top, po, ps, o_in, st_in, lg,
-           loc_sem, kv_send, kv_recv, send, recv):
+def kernel(host_in, len_in, q_ref, k_ref, v_ref, out_ref, log_ref,
+           host_ref, len_ref, kv, s1a, s1b, x2a, x2b, s2a, s2b, qg, qm, acc, top, po, ps, o_in, st_in,
+           oa, ob, lg, loc_sem, kv_send, kv_recv, send, recv):
     me = lax.axis_index("ctx")
     x, z, y = me // 32, (me // 4) % 8, me % 4
     xy = x * 4 + y
@@ -69,7 +69,14 @@
     def b_chunk(zz):
         return q_ref.at[rows((zz // 2) * 16, 16), cols(A_COLS + lax.rem(zz, 2) * 1024, 1024)]
 
+    barrier = pltpu.get_barrier_semaphore()
+    for k in range(1, NZ):
+        pl.semaphore_signal(barrier, inc=1, device_id=at_z(z_of(k)), device_id_type=MESH)
+    for k in range(1, NXY):
+        pl.semaphore_signal(barrier, inc=1, device_id=xy_to(k)[1], device_id_type=MESH)
     local = [
+        pltpu.make_async_copy(len_in, len_ref, loc_sem.at[4]),
+        pltpu.make_async_copy(host_in, host_ref, loc_sem.at[5]),
         pltpu.make_async_copy(k_ref, kv.at[xy, pl.ds(0, KEYS)], loc_sem.at[0]),
         pltpu.make_async_copy(v_ref, kv.at[xy, pl.ds(KEYS, KEYS)], loc_sem.at[1]),
         pltpu.make_async_copy(a_chunk(xy), s1a.at[xy], loc_sem.at[2]),
@@ -77,38 +84,62 @@
     ]
     for copy in local:
         copy.start()
-
-    barrier = pltpu.get_barrier_semaphore()
-    for k in range(1, NZ):
-        pl.semaphore_signal(barrier, inc=1, device_id=at_z(z_of(k)), device_id_type=MESH)
-    for k in range(1, NXY):
-        pl.semaphore_signal(barrier, inc=1, device_id=xy_to(k)[1], device_id_type=MESH)
+    local[0].wait()
     length = len_ref[0, 0].astype(jnp.float32)
     kv[xy, 2 * KEYS:, :] = jnp.full((16, DH), length, jnp.float32).astype(jnp.bfloat16)
-    pl.semaphore_wait(barrier, 14)
-
-    for k in xy_order:
-        c, device = xy_to(k)
-        put(a_chunk(c), s1a.at[xy], 0, device)
-    for k in z_order:
-        zz = z_of(k)
-        put(b_chunk(zz), s1b.at[z], 1, at_z(zz))
-    local[0].wait()
     local[1].wait()
-
-    def kv_copy(k):
-        return pltpu.make_async_remote_copy(
-            src_ref=kv.at[xy], dst_ref=kv.at[xy], send_sem=kv_send.at[k], recv_sem=kv_recv.at[k],
-            device_id=xy_to(k)[1], device_id_type=MESH)
-
-    for k in range(1, NXY):
-        kv_copy(k).start()
-
     host = host_ref[0]
     host_z = lax.rem(host // 4, 8)
     host_xy = host // 32 * 4 + lax.rem(host, 4)
-
+    pl.semaphore_wait(barrier, 14)
+
+    for k in xy_order:
+        c, device = xy_to(k)
+        put(a_chunk(c), s1a.at[xy], 0, device)
+    for k in z_order:
+        zz = z_of(k)
+        put(b_chunk(zz), s1b.at[z], 1, at_z(zz))
     local[2].wait()
+    local[3].wait()
+    up, down, over = lax.rem(y + 1, 4), lax.rem(y + 3, 4), 1 - x
+    far = lax.rem(y + 2, 4)
+    to_up = {"ctx": x * 32 + z * 4 + up}
+    to_down = {"ctx": x * 32 + z * 4 + down}
+    to_over = {"ctx": over * 32 + z * 4 + y}
+    whole, k_half, v_half = (0, 2 * KEYS + 16), (0, KEYS), (KEYS, KEYS + 16)
+
+    def kv_copy(slot, part, sem, device):
+        ref = kv.at[slot, pl.ds(*part)]
+        return pltpu.make_async_remote_copy(
+            src_ref=ref, dst_ref=ref, send_sem=kv_send.at[sem], recv_sem=kv_recv.at[sem],
+            device_id=device, device_id_type=MESH)
+
+    kv_sent = [
+        kv_copy(xy, whole, 0, to_over),
+        kv_copy(xy, whole, 1, to_up),
+        kv_copy(xy, whole, 2, to_down),
+        kv_copy(over * 4 + y, whole, 3, to_up),
+        kv_copy(over * 4 + y, whole, 4, to_down),
+        kv_copy(x * 4 + down, k_half, 5, to_up),
+        kv_copy(x * 4 + up, v_half, 6, to_down),
+        kv_copy(over * 4 + down, k_half, 7, to_up),
+        kv_copy(over * 4 + up, v_half, 8, to_down),
+    ]
+    kv_got = [
+        kv_copy(over * 4 + y, whole, 0, to_over),
+        kv_copy(x * 4 + down, whole, 1, to_up),
+        kv_copy(x * 4 + up, whole, 2, to_down),
+        kv_copy(over * 4 + down, whole, 3, to_up),
+        kv_copy(over * 4 + up, whole, 4, to_down),
+        kv_copy(x * 4 + far, k_half, 5, to_up),
+        kv_copy(x * 4 + far, v_half, 6, to_down),
+        kv_copy(over * 4 + far, k_half, 7, to_up),
+        kv_copy(over * 4 + far, v_half, 8, to_down),
+    ]
+    for n in range(3):
+        kv_sent[n].start()
+
+    local[4].wait()
     both(0, s1a.at[pl.ds(0, 7)]).wait_recv()
     chunk = s1a[host_xy]
     for p in range(NZ):
@@ -118,7 +149,7 @@
     for k in z_order:
         zz = z_of(k)
         put(x2a.at[zz], s2a.at[z], 2, at_z(zz))
-    local[3].wait()
+    local[5].wait()
     both(1, s1b.at[pl.ds(0, 7)]).wait_recv()
     chunk = s1b[host_z]
     for p in range(NXY):
@@ -128,12 +159,24 @@
         c, device = xy_to(k)
         put(x2b.at[c], s2b.at[xy], 3, device)
 
+    kv_got[0].wait_recv()
+    kv_sent[3].start()
+    kv_sent[4].start()
+    kv_got[1].wait_recv()
+    kv_sent[5].start()
+    kv_got[2].wait_recv()
+    kv_sent[6].start()
+
     both(2, s2a.at[pl.ds(0, 7)]).wait_recv()
     both(3, s2b.at[pl.ds(0, 7)]).wait_recv()
     qg[z, :, 0:256] = s2a[host_z]
     qg[z, :, 256:384] = s2b[host_xy]
     for k in z_order:
         put(qg.at[z], qg.at[z], 4, at_z(z_of(k)))
+    kv_got[3].wait_recv()
+    kv_sent[7].start()
+    kv_got[4].wait_recv()
+    kv_sent[8].start()
     both(4, qg.at[pl.ds(0, 7)]).wait_recv()
     for p in range(NZ):
         for c in range(3):
@@ -159,16 +202,17 @@
         top[...] = jnp.broadcast_to(new, top.shape)
 
     attend(xy)
-
-    def step(k, carry):
-        c = lax.rem(x + k // 4, 2) * 4 + lax.rem(y - lax.rem(k, 4) + 4, 4)
-        pltpu.make_async_remote_copy(
-            src_ref=kv.at[c], dst_ref=kv.at[c], send_sem=kv_send.at[k], recv_sem=kv_recv.at[k],
-            device_id=at_z(z_of(1)), device_id_type=MESH).wait_recv()
-        attend(c)
-        return carry
-
-    lax.fori_loop(1, NXY, step, 0)
+    attend(over * 4 + y)
+    attend(x * 4 + down)
+    attend(x * 4 + up)
+    attend(over * 4 + down)
+    attend(over * 4 + up)
+    kv_got[5].wait_recv()
+    kv_got[6].wait_recv()
+    attend(x * 4 + far)
+    kv_got[7].wait_recv()
+    kv_got[8].wait_recv()
+    attend(over * 4 + far)
 
     total = acc[:, DH:]
     po[...] = (acc[:, :DH] / total).astype(jnp.bfloat16).reshape(NZ, PIECE, DH)
@@ -199,25 +243,29 @@
     result = result.astype(jnp.bfloat16)
 
     mine = rows(tg * 16, 16)
-    a_here = out_ref.at[mine, cols(xy * 512 + hg * 256, 256)]
-    b_here = out_ref.at[mine, cols(A_COLS + hg * 1024 + xy * 128, 128)]
-    out_ref[mine, cols(xy * 512 + hg * 256, 128)] = result[0:16]
-    out_ref[mine, cols(xy * 512 + hg * 256 + 128, 128)] = result[16:32]
-    out_ref[mine, cols(A_COLS + hg * 1024 + xy * 128, 128)] = result[32:48]
-    for k in z_order:
-        put(a_here, a_here, 7, at_z(z_of(k)))
-    for k in xy_order:
-        put(b_here, b_here, 8, xy_to(k)[1])
+    oa_mine = oa.at[mine, cols(hg * 256, 256)]
+    ob_mine = ob.at[:, cols(xy * 128, 128)]
+    oa[mine, cols(hg * 256, 128)] = result[0:16]
+    oa[mine, cols(hg * 256 + 128, 128)] = result[16:32]
+    ob[:, cols(xy * 128, 128)] = result[32:48]
+    for k in z_order:
+        put(oa_mine, oa_mine, 7, at_z(z_of(k)))
+    for k in xy_order:
+        put(ob_mine, ob_mine, 8, xy_to(k)[1])
     for k in z_order:
         put(lg.at[xy, z], lg.at[xy, z], 9, at_z(z_of(k)))
+    a_out = out_ref.at[:, cols(xy * 512, 512)]
+    b_out = out_ref.at[mine, cols(A_COLS + hg * 1024, 1024)]
     both(7, s2a.at[pl.ds(0, 7)]).wait_recv()
-    a_all = out_ref.at[:, cols(xy * 512, 512)]
-    for k in xy_order:
-        put(a_all, a_all, 10, xy_to(k)[1])
+    for k in xy_order:
+        put(oa, a_out, 10, xy_to(k)[1])
+    keep_a = pltpu.make_async_copy(oa, a_out, loc_sem.at[0])
+    keep_a.start()
     both(8, s2b.at[pl.ds(0, 7)]).wait_recv()
-    b_all = out_ref.at[mine, cols(A_COLS + hg * 1024, 1024)]
-    for k in z_order:
-        put(b_all, b_all, 11, at_z(z_of(k)))
+    for k in z_order:
+        put(ob, b_out, 11, at_z(z_of(k)))
+    keep_b = pltpu.make_async_copy(ob, b_out, loc_sem.at[1])
+    keep_b.start()
     both(9, st_in.at[pl.ds(0, 7)]).wait_recv()
     for k in xy_order:
         put(lg.at[xy], lg.at[xy], 12, xy_to(k)[1])
@@ -239,8 +287,10 @@
     both(11, s1b.at[pl.ds(0, 7)]).wait_recv()
     for stage, like in enumerate((s1a, s1b, s2a, s2b, qg, o_in, st_in, s2a, s2b, st_in, s1a, s1b, lg)):
         both(stage, like.at[pl.ds(0, 7)]).wait_send()
-    for k in range(1, NXY):
-        kv_copy(k).wait_send()
+    for copy in kv_sent:
+        copy.wait_send()
+    keep_a.wait()
+    keep_b.wait()
 
 
 def body(queries, keys, values, query_host, lengths):
@@ -252,17 +302,19 @@
             jax.ShapeDtypeStruct((1, H), f32),
         ),
         in_specs=[
-            pl.BlockSpec(memory_space=pltpu.SMEM),
-            pl.BlockSpec(memory_space=pltpu.SMEM),
+            pl.BlockSpec(memory_space=pl.ANY),
+            pl.BlockSpec(memory_space=pl.ANY),
             pl.BlockSpec(memory_space=pl.ANY),
             pl.BlockSpec(memory_space=pl.ANY),
             pl.BlockSpec(memory_space=pl.ANY),
         ],
         out_specs=(
-            pl.BlockSpec(memory_space=pltpu.VMEM),
+            pl.BlockSpec(memory_space=pl.ANY),
             pl.BlockSpec(memory_space=pltpu.VMEM),
         ),
         scratch_shapes=[
+            pltpu.SMEM((1,), jnp.int32),
+            pltpu.SMEM((1, 1), jnp.int32),
             pltpu.VMEM((NXY, 2 * KEYS + 16, DH), bf16),
             pltpu.VMEM((NXY, T, 512), bf16),
             pltpu.VMEM((NZ, 16, 1024), bf16),
@@ -278,15 +330,17 @@
             pltpu.VMEM((NZ, 1, DH), f32),
             pltpu.VMEM((NZ, PIECE, DH), bf16),
             pltpu.VMEM((NZ, 1, DH), f32),
+            pltpu.VMEM((T, 512), bf16),
+            pltpu.VMEM((16, 1024), bf16),
             pltpu.VMEM((NXY, NZ, 1, DH), f32),
-            pltpu.SemaphoreType.DMA((4,)),
-            pltpu.SemaphoreType.DMA((NXY,)),
-            pltpu.SemaphoreType.DMA((NXY,)),
+            pltpu.SemaphoreType.DMA((6,)),
+            pltpu.SemaphoreType.DMA((9,)),
+            pltpu.SemaphoreType.DMA((9,)),
             pltpu.SemaphoreType.DMA((13,)),
             pltpu.SemaphoreType.DMA((13,)),
         ],
         compiler_params=pltpu.CompilerParams(
-            collective_id=0, has_side_effects=True, vmem_limit_bytes=40 * 2**20),
+            collective_id=0, has_side_effects=True, vmem_limit_bytes=60 * 2**20),
     )(query_host, lengths, queries.reshape(T, HD), keys.reshape(KEYS, DH), values.reshape(KEYS, DH))
     return attended[None], log_total[None]
 

time: 79.3 us -> 61 us (0.77)
  Pallas kernels: 72.3 us -> 56 us
  local copies, waits for them, and re-layouts: 4.33 us -> 2.58 us
    pallas_call x1, Pallas kernels: 72.3 us -> 56 us  [body(): pl.pallas_call(kernel, out_shape=(jax.ShapeDtypeStruct((T, HD), bf16), ja...]
    unnamed x8 -> x4, local copies, waits for them, and re-layouts: 4.33 us -> 2.58 us
where the time goes in v2:
time: 61 us; the launch traced here: 60.5 us
  Pallas kernels  56 us (92%)
  local copies, waits for them, and re-layouts  2.58 us (4%)
  between operations  1.94 us (3%)
    pallas_call x1, Pallas kernels, body(): pl.pallas_call(kernel, out_shape=(jax.ShapeDtypeStruct((T, HD), bf16), ja...  56 us
    unnamed x4, local copies, waits for them, and re-layouts  2.58 us

profile of v2, /device:TPU:2, one launch (start us, length us, event | category | flops | bytes accessed | tf_op | source)
XLA Modules:
  0.0 60.5 jit_solution(2151365174151429928)
XLA Ops:
  1.9 56.0 %shard_map.68 = (bf16[64,6144]{1,0:T(8,128)(2,1)}, f32[1,48]{1,0:T(1,128)}) custom-call(s32[1]{0:T(128)S(6)} %copy.9.host_in, s32[1,1]{1,0:T(1,128)S(6)} %copy.10.len_in, bf16[64,6144]{1,0:T(8,128)(2,1)} %bitcast.5, bf16[512,128]{1,0:T(8,128)(2,1)} %bitcast.7, bf16[512,128]{1,0:T(8,128)(2,1)} %bitcast.8), custom_call_target="tpu_custom_call" | custom-call | tf_op jit(solution)/shard_map/pallas_call | solution.py:298
  57.9 0.0 copy-start
  57.9 2.1 %copy.11 = bf16[1,64,6144]{2,1,0:T(8,128)(2,1)} copy(bf16[1,64,6144]{2,1,0:T(8,128)(2,1)} %bitcast.6) | data formatting | bytes 1572864
  60.0 0.0 copy-done
  60.0 0.5 copy.12
Async XLA Ops:
  57.9 2.1 %copy-start = (f32[1,48]{1,0:T(1,128)S(1)}, f32[1,48]{1,0:T(1,128)}, u32[]{:S(2)}) copy-start(f32[1,48]{1,0:T(1,128)} %get-tuple-element.5) | copy-start | bytes 580

commit v3 on v2

v3 whole, which is shorter than its diff:
```python
import math

import jax
import jax.numpy as jnp
from jax import lax
from jax.experimental import pallas as pl
from jax.experimental.pallas import tpu as pltpu
from jax.sharding import PartitionSpec as P


H = 48
DH = 128
T = 64
KEYS = 512
BLOCK = 128
HD = H * DH
NZ = 8
NXY = 8
ROWS = 384
OWN = 16
PIECE = 48
A_COLS = 4096
NEG = -1e30
LOG2E = math.log2(math.e)
LN2 = math.log(2.0)
SCALE = DH ** -0.5 * LOG2E
MESH = pl.DeviceIdType.MESH


def kernel(host_in, len_in, q_ref, k_ref, v_ref, out_ref, log_ref,
           host_ref, len_ref, kv, s1a, s1b, x2a, x2b, s2a, s2b, qg, qm, acc, po, ps, o_in, st_in,
           oa, ob, lg, loc_sem, kv_send, kv_recv, send, recv):
    me = lax.axis_index("ctx")
    x, z, y = me // 32, (me // 4) % 8, me % 4
    xy = x * 4 + y
    tg, hg = z // 2, z % 2
    mine_kv, over_kv = x * 2 + y % 2, (1 - x) * 2 + y % 2

    def z_of(k):
        return lax.rem(z + k, NZ)

    def at_z(zz):
        return {"ctx": x * 32 + zz * 4 + y}

    def owner_to(k):
        zz = z_of(k % NZ)
        return zz + k // NZ * NZ, {"ctx": x * 32 + zz * 4 + (y if k < NZ else 3 - y)}

    def xy_to(k):
        px, py = lax.rem(x + k // 4, 2), lax.rem(y + k % 4, 4)
        return px * 4 + py, {"ctx": px * 32 + z * 4 + py}

    def put(src, dst, stage, device):
        pltpu.make_async_remote_copy(
            src_ref=src, dst_ref=dst, send_sem=send.at[stage], recv_sem=recv.at[stage],
            device_id=device, device_id_type=MESH).start()

    def both(stage, like):
        return pltpu.make_async_remote_copy(
            src_ref=like, dst_ref=like, send_sem=send.at[stage], recv_sem=recv.at[stage],
            device_id=at_z(z_of(1)), device_id_type=MESH)

    def cols(start, n):
        return pl.ds(pl.multiple_of(start, 128), n)

    def rows(start, n):
        return pl.ds(pl.multiple_of(start, 16), n)

    z_order = (4, 3, 5, 2, 6, 1, 7)
    xy_order = (6, 5, 7, 2, 4, 1, 3)
    owner_order = (12, 4, 11, 13, 3, 5, 10, 14, 2, 6, 9, 15, 1, 7, 8)

    def a_chunk(c):
        return q_ref.at[:, cols(c * 512, 512)]

    def b_chunk(zz):
        return q_ref.at[rows((zz // 2) * 16, 16), cols(A_COLS + lax.rem(zz, 2) * 1024, 1024)]

    barrier = pltpu.get_barrier_semaphore()
    for k in range(1, NZ):
        pl.semaphore_signal(barrier, inc=1, device_id=at_z(z_of(k)), device_id_type=MESH)
    for k in range(1, NXY):
        pl.semaphore_signal(barrier, inc=1, device_id=xy_to(k)[1], device_id_type=MESH)
    for k in range(9, 16):
        pl.semaphore_signal(barrier, inc=1, device_id=owner_to(k)[1], device_id_type=MESH)
    local = [
        pltpu.make_async_copy(len_in, len_ref, loc_sem.at[4]),
        pltpu.make_async_copy(host_in, host_ref, loc_sem.at[5]),
        pltpu.make_async_copy(k_ref, kv.at[mine_kv, pl.ds(0, KEYS)], loc_sem.at[0]),
        pltpu.make_async_copy(v_ref, kv.at[mine_kv, pl.ds(KEYS, KEYS)], loc_sem.at[1]),
        pltpu.make_async_copy(a_chunk(xy), s1a.at[xy], loc_sem.at[2]),
        pltpu.make_async_copy(b_chunk(z), s1b.at[z], loc_sem.at[3]),
    ]
    for copy in local:
        copy.start()
    local[0].wait()
    length = len_ref[0, 0].astype(jnp.float32)
    kv[mine_kv, 2 * KEYS:, :] = jnp.full((16, DH), length, jnp.float32).astype(jnp.bfloat16)
    local[1].wait()
    host = host_ref[0]
    host_z = lax.rem(host // 4, 8)
    host_xy = host // 32 * 4 + lax.rem(host, 4)
    pl.semaphore_wait(barrier, 21)

    for k in xy_order:
        c, device = xy_to(k)
        put(a_chunk(c), s1a.at[xy], 0, device)
    for k in z_order:
        zz = z_of(k)
        put(b_chunk(zz), s1b.at[z], 1, at_z(zz))
    local[2].wait()
    local[3].wait()
    over = {"ctx": (1 - x) * 32 + z * 4 + y}
    pair = {"ctx": x * 32 + z * 4 + y + 1 - y % 2 * 2}

    def kv_copy(slot, sem, device):
        return pltpu.make_async_remote_copy(
            src_ref=kv.at[slot], dst_ref=kv.at[slot], send_sem=kv_send.at[sem], recv_sem=kv_recv.at[sem],
            device_id=device, device_id_type=MESH)

    kv_sent = [kv_copy(mine_kv, 0, over), kv_copy(mine_kv, 1, pair), kv_copy(over_kv, 2, pair)]
    kv_got = [
        kv_copy(over_kv, 0, over),
        kv_copy(x * 2 + 1 - y % 2, 1, pair),
        kv_copy((1 - x) * 2 + 1 - y % 2, 2, pair),
    ]
    kv_sent[0].start()
    kv_sent[1].start()

    local[4].wait()
    both(0, s1a.at[pl.ds(0, 7)]).wait_recv()
    chunk = s1a[host_xy]
    for p in range(NZ):
        a, b = p // 2, p % 2
        x2a[p] = chunk[16 * a:16 * a + 16, 256 * b:256 * b + 256]
    s2a[z] = x2a[z]
    for k in z_order:
        zz = z_of(k)
        put(x2a.at[zz], s2a.at[z], 2, at_z(zz))
    local[5].wait()
    both(1, s1b.at[pl.ds(0, 7)]).wait_recv()
    chunk = s1b[host_z]
    for p in range(NXY):
        x2b[p] = chunk[:, 128 * p:128 * p + 128]
    s2b[xy] = x2b[xy]
    for k in xy_order:
        c, device = xy_to(k)
        put(x2b.at[c], s2b.at[xy], 3, device)

    kv_got[0].wait_recv()
    kv_sent[2].start()

    both(2, s2a.at[pl.ds(0, 7)]).wait_recv()
    both(3, s2b.at[pl.ds(0, 7)]).wait_recv()
    qg[z, :, 0:256] = s2a[host_z]
    qg[z, :, 256:384] = s2b[host_xy]
    for k in owner_order:
        n, device = owner_to(k)
        put(qg.at[z], qg.at[z + k // NZ * NZ], 4, device)
    kv_got[1].wait_recv()
    kv_got[2].wait_recv()

    block_id = (lax.broadcasted_iota(jnp.int32, (1, KEYS), 1) // BLOCK).astype(jnp.float32)
    lane = lax.broadcasted_iota(jnp.int32, (PIECE, DH), 1)
    diagonal = lane == lax.broadcasted_iota(jnp.int32, (PIECE, DH), 0)
    both(4, qg.at[pl.ds(0, OWN - 1)]).wait_recv()

    def attend(half):
        for p in range(NZ):
            for c in range(3):
                qm[half, PIECE * p + 16 * c:PIECE * p + 16 * c + 16, :] = (
                    qg[half * NZ + p, :, 128 * c:128 * c + 128])
        old = total = None
        for c in range(4):
            valid = kv[c, 2 * KEYS:2 * KEYS + 16, :].astype(jnp.float32)[0:1, :]
            valid = jnp.concatenate([valid] * (KEYS // DH), axis=1)
            score = lax.dot_general(
                qm[half], kv[c, 0:KEYS, :], (((1,), (1,)), ((), ())), preferred_element_type=jnp.float32)
            score = jnp.where(block_id < valid, score * SCALE, NEG)
            new = jnp.max(score, axis=1, keepdims=True)
            if c:
                new = jnp.maximum(old, new)
            weight = jnp.exp2(score - new).astype(jnp.bfloat16)
            value = jnp.concatenate(
                [kv[c, KEYS:2 * KEYS, :], jnp.ones((KEYS, DH), jnp.bfloat16)], axis=1)
            summed = jnp.dot(weight, value, preferred_element_type=jnp.float32)
            acc[half] = acc[half] * jnp.exp2(old - new) + summed if c else summed
            old = new
        total = acc[half, :, DH:]
        po[half * NZ:half * NZ + NZ] = (
            acc[half, :, :DH] / total).astype(jnp.bfloat16).reshape(NZ, PIECE, DH)
        lse = old + jnp.log(total) * LOG2E
        for p in range(NZ):
            part = lse[PIECE * p:PIECE * p + PIECE, :]
            ps[half * NZ + p] = jnp.sum(jnp.where(diagonal, part, 0.0), axis=0, keepdims=True)
        if half == 0:
            o_in[z] = po[z]
            st_in[z] = ps[z]
        for k in owner_order:
            if k // NZ == half:
                n, device = owner_to(k)
                put(po.at[n], o_in.at[half * NZ + z], 5, device)
                put(ps.at[n], st_in.at[half * NZ + z], 6, device)

    attend(1)
    attend(0)
    both(6, st_in.at[pl.ds(0, OWN - 1)]).wait_recv()
    stat = jnp.concatenate([st_in[s] for s in range(OWN)], axis=0)
    overall = jnp.max(stat, axis=0, keepdims=True)
    share = jnp.exp2(stat - overall)
    summed = jnp.sum(share, axis=0, keepdims=True)
    share = share / summed
    lg[xy, z] = overall * LN2 + jnp.log(summed)
    both(5, o_in.at[pl.ds(0, OWN - 1)]).wait_recv()
    result = jnp.zeros((PIECE, DH), jnp.float32)
    for s in range(OWN):
        column = jnp.sum(jnp.where(diagonal, share[s:s + 1, :], 0.0), axis=1, keepdims=True)
        result = result + column * o_in[s].astype(jnp.float32)
    result = result.astype(jnp.bfloat16)

    mine = rows(tg * 16, 16)
    oa_mine = oa.at[mine, cols(hg * 256, 256)]
    ob_mine = ob.at[:, cols(xy * 128, 128)]
    oa[mine, cols(hg * 256, 128)] = result[0:16]
    oa[mine, cols(hg * 256 + 128, 128)] = result[16:32]
    ob[:, cols(xy * 128, 128)] = result[32:48]
    for k in z_order:
        put(oa_mine, oa_mine, 7, at_z(z_of(k)))
    for k in xy_order:
        put(ob_mine, ob_mine, 8, xy_to(k)[1])
    for k in z_order:
        put(lg.at[xy, z], lg.at[xy, z], 9, at_z(z_of(k)))
    a_out = out_ref.at[:, cols(xy * 512, 512)]
    b_out = out_ref.at[mine, cols(A_COLS + hg * 1024, 1024)]
    both(7, s2a.at[pl.ds(0, 7)]).wait_recv()
    for k in xy_order:
        put(oa, a_out, 10, xy_to(k)[1])
    keep_a = pltpu.make_async_copy(oa, a_out, loc_sem.at[0])
    keep_a.start()
    both(8, s2b.at[pl.ds(0, 7)]).wait_recv()
    for k in z_order:
        put(ob, b_out, 11, at_z(z_of(k)))
    keep_b = pltpu.make_async_copy(ob, b_out, loc_sem.at[1])
    keep_b.start()
    both(9, ps.at[pl.ds(0, 7)]).wait_recv()
    for k in xy_order:
        put(lg.at[xy], lg.at[xy], 12, xy_to(k)[1])

    both(12, lg.at[pl.ds(0, 7)]).wait_recv()
    t_group, t_in = me // 16, lax.rem(me, 16)
    lane = lax.broadcasted_iota(jnp.int32, (NXY, DH), 1)
    source = lax.broadcasted_iota(jnp.int32, (NXY, DH), 0)
    logs = jnp.zeros((NXY, DH), jnp.float32)
    for b in range(2):
        part = jnp.concatenate([lg[c, 2 * t_group + b] for c in range(NXY)], axis=0)
        for c in range(3):
            column = jnp.sum(jnp.where(lane == 16 * c + t_in, part, 0.0), axis=1, keepdims=True)
            head = source * 4 + 2 * b + c if c < 2 else 32 + 8 * b + source
            logs = logs + jnp.where(lane == head, column, 0.0)
    log_ref[...] = jnp.sum(logs, axis=0, keepdims=True)[:, :H]

    both(10, s1a.at[pl.ds(0, 7)]).wait_recv()
    both(11, s1b.at[pl.ds(0, 7)]).wait_recv()
    for stage, like in enumerate((s1a, s1b, s2a, s2b, None, None, None, s2a, s2b, ps, s1a, s1b, lg)):
        if like is not None:
            both(stage, like.at[pl.ds(0, 7)]).wait_send()
    for stage, like in ((4, qg), (5, o_in), (6, st_in)):
        both(stage, like.at[pl.ds(0, OWN - 1)]).wait_send()
    for copy in kv_sent:
        copy.wait_send()
    keep_a.wait()
    keep_b.wait()


def body(queries, keys, values, query_host, lengths):
    bf16, f32 = jnp.bfloat16, jnp.float32
    attended, log_total = pl.pallas_call(
        kernel,
        out_shape=(
            jax.ShapeDtypeStruct((T, HD), bf16),
            jax.ShapeDtypeStruct((1, H), f32),
        ),
        in_specs=[
            pl.BlockSpec(memory_space=pl.ANY),
            pl.BlockSpec(memory_space=pl.ANY),
            pl.BlockSpec(memory_space=pl.ANY),
            pl.BlockSpec(memory_space=pl.ANY),
            pl.BlockSpec(memory_space=pl.ANY),
        ],
        out_specs=(
            pl.BlockSpec(memory_space=pl.ANY),
            pl.BlockSpec(memory_space=pltpu.VMEM),
        ),
        scratch_shapes=[
            pltpu.SMEM((1,), jnp.int32),
            pltpu.SMEM((1, 1), jnp.int32),
            pltpu.VMEM((4, 2 * KEYS + 16, DH), bf16),
            pltpu.VMEM((NXY, T, 512), bf16),
            pltpu.VMEM((NZ, 16, 1024), bf16),
            pltpu.VMEM((NZ, 16, 256), bf16),
            pltpu.VMEM((NXY, 16, 128), bf16),
            pltpu.VMEM((NZ, 16, 256), bf16),
            pltpu.VMEM((NXY, 16, 128), bf16),
            pltpu.VMEM((OWN, 16, 384), bf16),
            pltpu.VMEM((2, ROWS, DH), bf16),
            pltpu.VMEM((2, ROWS, 2 * DH), f32),
            pltpu.VMEM((OWN, PIECE, DH), bf16),
            pltpu.VMEM((OWN, 1, DH), f32),
            pltpu.VMEM((OWN, PIECE, DH), bf16),
            pltpu.VMEM((OWN, 1, DH), f32),
            pltpu.VMEM((T, 512), bf16),
            pltpu.VMEM((16, 1024), bf16),
            pltpu.VMEM((NXY, NZ, 1, DH), f32),
            pltpu.SemaphoreType.DMA((6,)),
            pltpu.SemaphoreType.DMA((3,)),
            pltpu.SemaphoreType.DMA((3,)),
            pltpu.SemaphoreType.DMA((13,)),
            pltpu.SemaphoreType.DMA((13,)),
        ],
        compiler_params=pltpu.CompilerParams(
            collective_id=0, has_side_effects=True, vmem_limit_bytes=60 * 2**20),
    )(query_host, lengths, queries.reshape(T, HD), keys.reshape(KEYS, DH), values.reshape(KEYS, DH))
    return attended[None], log_total[None]


def solution(mesh):
    return jax.shard_map(
        body,
        mesh=mesh,
        in_specs=(
            P("req", "ctx", None, None),
            P("req", "ctx", None),
            P("req", "ctx", None),
            P("req"),
            P("req", "ctx"),
        ),
        out_specs=(P("req", None, None), P("req", "ctx", None)),
        check_vma=False,
    )
```

time: 61 us -> 57.1 us (0.936)
  Pallas kernels: 56 us -> 51.9 us
    pallas_call x1, Pallas kernels: 56 us -> 51.9 us  [body(): pl.pallas_call(kernel, out_shape=(jax.ShapeDtypeStruct((T, HD), bf16), ja...]
where the time goes in v3:
time: 57.1 us; the launch traced here: 56.4 us
  Pallas kernels  51.9 us (91%)
  local copies, waits for them, and re-layouts  2.58 us (5%)
  between operations  1.94 us (3%)
    pallas_call x1, Pallas kernels, body(): pl.pallas_call(kernel, out_shape=(jax.ShapeDtypeStruct((T, HD), bf16), ja...  51.9 us
    unnamed x4, local copies, waits for them, and re-layouts  2.58 us

profile of v3, /device:TPU:2, one launch (start us, length us, event | category | flops | bytes accessed | tf_op | source)
XLA Modules:
  0.0 56.4 jit_solution(13899335739483872135)
XLA Ops:
  1.9 51.9 %shard_map.68 = (bf16[64,6144]{1,0:T(8,128)(2,1)}, f32[1,48]{1,0:T(1,128)}) custom-call(s32[1]{0:T(128)S(6)} %copy.9.host_in, s32[1,1]{1,0:T(1,128)S(6)} %copy.10.len_in, bf16[64,6144]{1,0:T(8,128)(2,1)} %bitcast.5, bf16[512,128]{1,0:T(8,128)(2,1)} %bitcast.7, bf16[512,128]{1,0:T(8,128)(2,1)} %bitcast.8), custom_call_target="tpu_custom_call" | custom-call | tf_op jit(solution)/shard_map/pallas_call | solution.py:277
  53.8 0.0 copy-start
  53.8 2.1 %copy.11 = bf16[1,64,6144]{2,1,0:T(8,128)(2,1)} copy(bf16[1,64,6144]{2,1,0:T(8,128)(2,1)} %bitcast.6) | data formatting | bytes 1572864
  55.9 0.0 copy-done
  55.9 0.5 copy.12
Async XLA Ops:
  53.8 2.1 %copy-start = (f32[1,48]{1,0:T(1,128)S(1)}, f32[1,48]{1,0:T(1,128)}, u32[]{:S(2)}) copy-start(f32[1,48]{1,0:T(1,128)} %get-tuple-element.5) | copy-start | bytes 580

commit v4 on v3

--- a/solution.py
+++ b/solution.py
@@ -27,9 +27,9 @@
 MESH = pl.DeviceIdType.MESH
 
 
-def kernel(host_in, len_in, q_ref, k_ref, v_ref, out_ref, log_ref,
+def kernel(host_in, len_in, q_ref, k_ref, v_ref, out_ref, log_out,
            host_ref, len_ref, kv, s1a, s1b, x2a, x2b, s2a, s2b, qg, qm, acc, po, ps, o_in, st_in,
-           oa, ob, lg, loc_sem, kv_send, kv_recv, send, recv):
+           oa, ob, lg, log_ref, loc_sem, kv_send, kv_recv, send, recv):
     me = lax.axis_index("ctx")
     x, z, y = me // 32, (me // 4) % 8, me % 4
     xy = x * 4 + y
@@ -77,11 +77,23 @@
         return q_ref.at[rows((zz // 2) * 16, 16), cols(A_COLS + lax.rem(zz, 2) * 1024, 1024)]
 
     barrier = pltpu.get_barrier_semaphore()
-    for k in range(1, NZ):
+    for k in (4, 3, 5):
         pl.semaphore_signal(barrier, inc=1, device_id=at_z(z_of(k)), device_id_type=MESH)
-    for k in range(1, NXY):
+    for k in (6, 5, 7):
         pl.semaphore_signal(barrier, inc=1, device_id=xy_to(k)[1], device_id_type=MESH)
-    for k in range(9, 16):
+    for k in ():
+        pl.semaphore_signal(barrier, inc=1, device_id=owner_to(k)[1], device_id_type=MESH)
+    for k in (2, 6):
+        pl.semaphore_signal(barrier, inc=1, device_id=at_z(z_of(k)), device_id_type=MESH)
+    for k in (2, 4, 1, 3):
+        pl.semaphore_signal(barrier, inc=1, device_id=xy_to(k)[1], device_id_type=MESH)
+    for k in ():
+        pl.semaphore_signal(barrier, inc=1, device_id=owner_to(k)[1], device_id_type=MESH)
+    for k in (1, 7):
+        pl.semaphore_signal(barrier, inc=1, device_id=at_z(z_of(k)), device_id_type=MESH)
+    for k in ():
+        pl.semaphore_signal(barrier, inc=1, device_id=xy_to(k)[1], device_id_type=MESH)
+    for k in ():
         pl.semaphore_signal(barrier, inc=1, device_id=owner_to(k)[1], device_id_type=MESH)
     local = [
         pltpu.make_async_copy(len_in, len_ref, loc_sem.at[4]),
@@ -93,21 +105,17 @@
     ]
     for copy in local:
         copy.start()
+    pl.semaphore_wait(barrier, 14)
+
+    for k in xy_order:
+        c, device = xy_to(k)
+        put(a_chunk(c), s1a.at[xy], 0, device)
+    for k in z_order:
+        zz = z_of(k)
+        put(b_chunk(zz), s1b.at[z], 1, at_z(zz))
     local[0].wait()
     length = len_ref[0, 0].astype(jnp.float32)
     kv[mine_kv, 2 * KEYS:, :] = jnp.full((16, DH), length, jnp.float32).astype(jnp.bfloat16)
-    local[1].wait()
-    host = host_ref[0]
-    host_z = lax.rem(host // 4, 8)
-    host_xy = host // 32 * 4 + lax.rem(host, 4)
-    pl.semaphore_wait(barrier, 21)
-
-    for k in xy_order:
-        c, device = xy_to(k)
-        put(a_chunk(c), s1a.at[xy], 0, device)
-    for k in z_order:
-        zz = z_of(k)
-        put(b_chunk(zz), s1b.at[z], 1, at_z(zz))
     local[2].wait()
     local[3].wait()
     over = {"ctx": (1 - x) * 32 + z * 4 + y}
@@ -127,6 +135,10 @@
     kv_sent[0].start()
     kv_sent[1].start()
 
+    local[1].wait()
+    host = host_ref[0]
+    host_z = lax.rem(host // 4, 8)
+    host_xy = host // 32 * 4 + lax.rem(host, 4)
     local[4].wait()
     both(0, s1a.at[pl.ds(0, 7)]).wait_recv()
     chunk = s1a[host_xy]
@@ -165,17 +177,19 @@
     diagonal = lane == lax.broadcasted_iota(jnp.int32, (PIECE, DH), 0)
     both(4, qg.at[pl.ds(0, OWN - 1)]).wait_recv()
 
-    def attend(half):
-        for p in range(NZ):
+    def attend(group, ks):
+        targets = [owner_to(k) for k in ks]
+        size = PIECE * len(ks)
+        for i, (n, _) in enumerate(targets):
             for c in range(3):
-                qm[half, PIECE * p + 16 * c:PIECE * p + 16 * c + 16, :] = (
-                    qg[half * NZ + p, :, 128 * c:128 * c + 128])
+                qm[group, PIECE * i + 16 * c:PIECE * i + 16 * c + 16, :] = qg[n, :, 128 * c:128 * c + 128]
         old = total = None
         for c in range(4):
             valid = kv[c, 2 * KEYS:2 * KEYS + 16, :].astype(jnp.float32)[0:1, :]
             valid = jnp.concatenate([valid] * (KEYS // DH), axis=1)
             score = lax.dot_general(
-                qm[half], kv[c, 0:KEYS, :], (((1,), (1,)), ((), ())), preferred_element_type=jnp.float32)
+                qm[group, 0:size, :], kv[c, 0:KEYS, :], (((1,), (1,)), ((), ())),
+                preferred_element_type=jnp.float32)
             score = jnp.where(block_id < valid, score * SCALE, NEG)
             new = jnp.max(score, axis=1, keepdims=True)
             if c:
@@ -184,26 +198,23 @@
             value = jnp.concatenate(
                 [kv[c, KEYS:2 * KEYS, :], jnp.ones((KEYS, DH), jnp.bfloat16)], axis=1)
             summed = jnp.dot(weight, value, preferred_element_type=jnp.float32)
-            acc[half] = acc[half] * jnp.exp2(old - new) + summed if c else summed
+            acc[group, 0:size, :] = acc[group, 0:size, :] * jnp.exp2(old - new) + summed if c else summed
             old = new
-        total = acc[half, :, DH:]
-        po[half * NZ:half * NZ + NZ] = (
-            acc[half, :, :DH] / total).astype(jnp.bfloat16).reshape(NZ, PIECE, DH)
+        total = acc[group, 0:size, DH:]
+        part = (acc[group, 0:size, :DH] / total).astype(jnp.bfloat16)
         lse = old + jnp.log(total) * LOG2E
-        for p in range(NZ):
-            part = lse[PIECE * p:PIECE * p + PIECE, :]
-            ps[half * NZ + p] = jnp.sum(jnp.where(diagonal, part, 0.0), axis=0, keepdims=True)
-        if half == 0:
-            o_in[z] = po[z]
-            st_in[z] = ps[z]
-        for k in owner_order:
-            if k // NZ == half:
-                n, device = owner_to(k)
-                put(po.at[n], o_in.at[half * NZ + z], 5, device)
-                put(ps.at[n], st_in.at[half * NZ + z], 6, device)
-
-    attend(1)
-    attend(0)
+        for i, (k, (n, device)) in enumerate(zip(ks, targets)):
+            at = slice(PIECE * i, PIECE * i + PIECE)
+            stat = jnp.sum(jnp.where(diagonal, lse[at, :], 0.0), axis=0, keepdims=True)
+            if k:
+                po[n], ps[n] = part[at, :], stat
+                put(po.at[n], o_in.at[k // NZ * NZ + z], 5, device)
+                put(ps.at[n], st_in.at[k // NZ * NZ + z], 6, device)
+            else:
+                o_in[z], st_in[z] = part[at, :], stat
+
+    for group, ks in enumerate(((12, 11, 13, 4), (10, 14, 3, 5), (9, 15, 2, 6), (8, 1, 7, 0))):
+        attend(group, ks)
     both(6, st_in.at[pl.ds(0, OWN - 1)]).wait_recv()
     stat = jnp.concatenate([st_in[s] for s in range(OWN)], axis=0)
     overall = jnp.max(stat, axis=0, keepdims=True)
@@ -211,6 +222,8 @@
     summed = jnp.sum(share, axis=0, keepdims=True)
     share = share / summed
     lg[xy, z] = overall * LN2 + jnp.log(summed)
+    for k in z_order:
+        put(lg.at[xy, z], lg.at[xy, z], 9, at_z(z_of(k)))
     both(5, o_in.at[pl.ds(0, OWN - 1)]).wait_recv()
     result = jnp.zeros((PIECE, DH), jnp.float32)
     for s in range(OWN):
@@ -228,8 +241,9 @@
         put(oa_mine, oa_mine, 7, at_z(z_of(k)))
     for k in xy_order:
         put(ob_mine, ob_mine, 8, xy_to(k)[1])
-    for k in z_order:
-        put(lg.at[xy, z], lg.at[xy, z], 9, at_z(z_of(k)))
+    both(9, ps.at[pl.ds(0, 7)]).wait_recv()
+    for k in xy_order:
+        put(lg.at[xy], lg.at[xy], 12, xy_to(k)[1])
     a_out = out_ref.at[:, cols(xy * 512, 512)]
     b_out = out_ref.at[mine, cols(A_COLS + hg * 1024, 1024)]
     both(7, s2a.at[pl.ds(0, 7)]).wait_recv()
@@ -242,9 +256,6 @@
         put(ob, b_out, 11, at_z(z_of(k)))
     keep_b = pltpu.make_async_copy(ob, b_out, loc_sem.at[1])
     keep_b.start()
-    both(9, ps.at[pl.ds(0, 7)]).wait_recv()
-    for k in xy_order:
-        put(lg.at[xy], lg.at[xy], 12, xy_to(k)[1])
 
     both(12, lg.at[pl.ds(0, 7)]).wait_recv()
     t_group, t_in = me // 16, lax.rem(me, 16)
@@ -258,6 +269,8 @@
             head = source * 4 + 2 * b + c if c < 2 else 32 + 8 * b + source
             logs = logs + jnp.where(lane == head, column, 0.0)
     log_ref[...] = jnp.sum(logs, axis=0, keepdims=True)[:, :H]
+    keep_log = pltpu.make_async_copy(log_ref, log_out, loc_sem.at[2])
+    keep_log.start()
 
     both(10, s1a.at[pl.ds(0, 7)]).wait_recv()
     both(11, s1b.at[pl.ds(0, 7)]).wait_recv()
@@ -270,6 +283,7 @@
         copy.wait_send()
     keep_a.wait()
     keep_b.wait()
+    keep_log.wait()
 
 
 def body(queries, keys, values, query_host, lengths):
@@ -289,7 +303,7 @@
         ],
         out_specs=(
             pl.BlockSpec(memory_space=pl.ANY),
-            pl.BlockSpec(memory_space=pltpu.VMEM),
+            pl.BlockSpec(memory_space=pl.ANY),
         ),
         scratch_shapes=[
             pltpu.SMEM((1,), jnp.int32),
@@ -302,8 +316,8 @@
             pltpu.VMEM((NZ, 16, 256), bf16),
             pltpu.VMEM((NXY, 16, 128), bf16),
             pltpu.VMEM((OWN, 16, 384), bf16),
-            pltpu.VMEM((2, ROWS, DH), bf16),
-            pltpu.VMEM((2, ROWS, 2 * DH), f32),
+            pltpu.VMEM((4, ROWS, DH), bf16),
+            pltpu.VMEM((4, ROWS, 2 * DH), f32),
             pltpu.VMEM((OWN, PIECE, DH), bf16),
             pltpu.VMEM((OWN, 1, DH), f32),
             pltpu.VMEM((OWN, PIECE, DH), bf16),
@@ -311,6 +325,7 @@
             pltpu.VMEM((T, 512), bf16),
             pltpu.VMEM((16, 1024), bf16),
             pltpu.VMEM((NXY, NZ, 1, DH), f32),
+            pltpu.VMEM((1, H), f32),
             pltpu.SemaphoreType.DMA((6,)),
             pltpu.SemaphoreType.DMA((3,)),
             pltpu.SemaphoreType.DMA((3,)),

time: 57.1 us -> 54.8 us (0.960)
  Pallas kernels: 51.9 us -> 50.1 us
    pallas_call x1, Pallas kernels: 51.9 us -> 50.1 us  [body(): pl.pallas_call(kernel, out_shape=(jax.ShapeDtypeStruct((T, HD), bf16), ja...]
where the time goes in v4:
time: 54.8 us; the launch traced here: 54.6 us
  Pallas kernels  50.1 us (91%)
  local copies, waits for them, and re-layouts  2.58 us (5%)
  between operations  1.94 us (4%)
    pallas_call x1, Pallas kernels, body(): pl.pallas_call(kernel, out_shape=(jax.ShapeDtypeStruct((T, HD), bf16), ja...  50.1 us
    unnamed x4, local copies, waits for them, and re-layouts  2.58 us

profile of v4, /device:TPU:2, one launch (start us, length us, event | category | flops | bytes accessed | tf_op | source)
XLA Modules:
  0.0 54.6 jit_solution(6298928184182197195)
XLA Ops:
  1.9 50.1 %shard_map.68 = (bf16[64,6144]{1,0:T(8,128)(2,1)}, f32[1,48]{1,0:T(1,128)}) custom-call(s32[1]{0:T(128)S(6)} %copy.9.host_in, s32[1,1]{1,0:T(1,128)S(6)} %copy.10.len_in, bf16[64,6144]{1,0:T(8,128)(2,1)} %bitcast.5, bf16[512,128]{1,0:T(8,128)(2,1)} %bitcast.7, bf16[512,128]{1,0:T(8,128)(2,1)} %bitcast.8), custom_call_target="tpu_custom_call" | custom-call | tf_op jit(solution)/shard_map/pallas_call | solution.py:291
  52.1 0.0 copy-start
  52.1 2.1 %copy.11 = bf16[1,64,6144]{2,1,0:T(8,128)(2,1)} copy(bf16[1,64,6144]{2,1,0:T(8,128)(2,1)} %bitcast.6) | data formatting | bytes 1572864
  54.1 0.0 copy-done
  54.1 0.5 copy.12
Async XLA Ops:
  52.1 2.1 %copy-start = (f32[1,48]{1,0:T(1,128)S(1)}, f32[1,48]{1,0:T(1,128)}, u32[]{:S(2)}) copy-start(f32[1,48]{1,0:T(1,128)} %get-tuple-element.5) | copy-start | bytes 580

commit v5 on v4

--- a/solution.py
+++ b/solution.py
@@ -272,18 +272,20 @@
     keep_log = pltpu.make_async_copy(log_ref, log_out, loc_sem.at[2])
     keep_log.start()
 
-    both(10, s1a.at[pl.ds(0, 7)]).wait_recv()
-    both(11, s1b.at[pl.ds(0, 7)]).wait_recv()
-    for stage, like in enumerate((s1a, s1b, s2a, s2b, None, None, None, s2a, s2b, ps, s1a, s1b, lg)):
+    for stage, like in enumerate((s1a, s1b, s2a, s2b, None, None, None, s2a, s2b, ps, None, None, lg)):
         if like is not None:
             both(stage, like.at[pl.ds(0, 7)]).wait_send()
     for stage, like in ((4, qg), (5, o_in), (6, st_in)):
         both(stage, like.at[pl.ds(0, OWN - 1)]).wait_send()
     for copy in kv_sent:
         copy.wait_send()
+    keep_log.wait()
     keep_a.wait()
     keep_b.wait()
-    keep_log.wait()
+    both(10, s1a.at[pl.ds(0, 7)]).wait_send()
+    both(11, s1b.at[pl.ds(0, 7)]).wait_send()
+    both(11, s1b.at[pl.ds(0, 7)]).wait_recv()
+    both(10, s1a.at[pl.ds(0, 7)]).wait_recv()
 
 
 def body(queries, keys, values, query_host, lengths):
@@ -333,8 +335,12 @@
             pltpu.SemaphoreType.DMA((13,)),
         ],
         compiler_params=pltpu.CompilerParams(
-            collective_id=0, has_side_effects=True, vmem_limit_bytes=60 * 2**20),
-    )(query_host, lengths, queries.reshape(T, HD), keys.reshape(KEYS, DH), values.reshape(KEYS, DH))
+            collective_id=0, has_side_effects=True, vmem_limit_bytes=40 * 2**20),
+    )(
+        query_host, lengths,
+        pltpu.with_memory_space_constraint(queries.reshape(T, HD), pltpu.HBM),
+        pltpu.with_memory_space_constraint(keys.reshape(KEYS, DH), pltpu.HBM),
+        pltpu.with_memory_space_constraint(values.reshape(KEYS, DH), pltpu.HBM))
     return attended[None], log_total[None]
 
 

time: 54.8 us -> 53.4 us (0.974)
  local copies, waits for them, and re-layouts: 2.58 us -> 1.39 us
    unnamed x4 -> x2, local copies, waits for them, and re-layouts: 2.58 us -> 1.39 us
where the time goes in v5:
time: 53.4 us; the launch traced here: 53.3 us
  Pallas kernels  50 us (94%)
  between operations  1.93 us (4%)
  local copies, waits for them, and re-layouts  1.39 us (3%)
    pallas_call x1, Pallas kernels, body(): pl.pallas_call(kernel, out_shape=(jax.ShapeDtypeStruct((T, HD), bf16), ja...  50 us
    unnamed x2, local copies, waits for them, and re-layouts  1.39 us

profile of v5, /device:TPU:2, one launch (start us, length us, event | category | flops | bytes accessed | tf_op | source)
XLA Modules:
  0.0 53.3 jit_solution(9096131933990893044)
XLA Ops:
  1.9 50.0 %shard_map.68 = (bf16[64,6144]{1,0:T(8,128)(2,1)S(1)}, f32[1,48]{1,0:T(1,128)S(1)}) custom-call(s32[1]{0:T(128)S(6)} %copy.9.host_in, s32[1,1]{1,0:T(1,128)S(6)} %copy.10.len_in, bf16[64,6144]{1,0:T(8,128)(2,1)} %bitcast.7, bf16[512,128]{1,0:T(8,128)(2,1)} %bitcast.8, bf16[512,128]{1,0:T(8,128)(2,1)} %bitcast.9), custom_call_target="tpu_custom_call" | custom-call | tf_op jit(solution)/shard_map/pallas_call | solution.py:293
  51.9 0.9 %copy.11 = bf16[1,64,6144]{2,1,0:T(8,128)(2,1)} copy(bf16[1,64,6144]{2,1,0:T(8,128)(2,1)S(1)} %bitcast.5) | data formatting | bytes 1572864
  52.8 0.5 copy.12

commit v6 on v5

--- a/solution.py
+++ b/solution.py
@@ -175,6 +175,10 @@
     block_id = (lax.broadcasted_iota(jnp.int32, (1, KEYS), 1) // BLOCK).astype(jnp.float32)
     lane = lax.broadcasted_iota(jnp.int32, (PIECE, DH), 1)
     diagonal = lane == lax.broadcasted_iota(jnp.int32, (PIECE, DH), 0)
+    valid = []
+    for c in range(4):
+        count = kv[c, 2 * KEYS:2 * KEYS + 16, :].astype(jnp.float32)[0:1, :]
+        valid.append(block_id < jnp.concatenate([count] * (KEYS // DH), axis=1))
     both(4, qg.at[pl.ds(0, OWN - 1)]).wait_recv()
 
     def attend(group, ks):
@@ -185,12 +189,10 @@
                 qm[group, PIECE * i + 16 * c:PIECE * i + 16 * c + 16, :] = qg[n, :, 128 * c:128 * c + 128]
         old = total = None
         for c in range(4):
-            valid = kv[c, 2 * KEYS:2 * KEYS + 16, :].astype(jnp.float32)[0:1, :]
-            valid = jnp.concatenate([valid] * (KEYS // DH), axis=1)
             score = lax.dot_general(
                 qm[group, 0:size, :], kv[c, 0:KEYS, :], (((1,), (1,)), ((), ())),
                 preferred_element_type=jnp.float32)
-            score = jnp.where(block_id < valid, score * SCALE, NEG)
+            score = jnp.where(valid[c], score * SCALE, NEG)
             new = jnp.max(score, axis=1, keepdims=True)
             if c:
                 new = jnp.maximum(old, new)

time: 53.4 us -> 53.5 us (level)
  no operation moved by 1% of the time
where the time goes in v6:
time: 53.5 us; the launch traced here: 53.4 us
  Pallas kernels  50.1 us (94%)
  between operations  1.93 us (4%)
  local copies, waits for them, and re-layouts  1.39 us (3%)
    pallas_call x1, Pallas kernels, body(): pl.pallas_call(kernel, out_shape=(jax.ShapeDtypeStruct((T, HD), bf16), ja...  50.1 us
    unnamed x2, local copies, waits for them, and re-layouts  1.39 us

profile of v6, /device:TPU:2, one launch (start us, length us, event | category | flops | bytes accessed | tf_op | source)
XLA Modules:
  0.0 53.4 jit_solution(1565072394641955189)
XLA Ops:
  1.9 50.1 %shard_map.68 = (bf16[64,6144]{1,0:T(8,128)(2,1)S(1)}, f32[1,48]{1,0:T(1,128)S(1)}) custom-call(s32[1]{0:T(128)S(6)} %copy.9.host_in, s32[1,1]{1,0:T(1,128)S(6)} %copy.10.len_in, bf16[64,6144]{1,0:T(8,128)(2,1)} %bitcast.7, bf16[512,128]{1,0:T(8,128)(2,1)} %bitcast.8, bf16[512,128]{1,0:T(8,128)(2,1)} %bitcast.9), custom_call_target="tpu_custom_call" | custom-call | tf_op jit(solution)/shard_map/pallas_call | solution.py:295
  52.0 0.9 %copy.11 = bf16[1,64,6144]{2,1,0:T(8,128)(2,1)} copy(bf16[1,64,6144]{2,1,0:T(8,128)(2,1)S(1)} %bitcast.5) | data formatting | bytes 1572864
  52.9 0.5 copy.12
